TPU v7x, 512 devices: a whole 4x4x16 slice. The times are simulated.
512 devices in a mesh: outer: 32 (over x, y, z_hi), inner: 16 (over z_lo, core).
Axes of the slice: x: 4, y: 4, z: 16 (z_hi: 2, z_lo: 8; z = z_hi * 8 + z_lo), core: 2. Of those that a mesh axis runs over, the one named last changes fastest.
Arguments:
- notes: bfloat16 [20480, 512], P('outer'), may hold values from -8 to 8
- timelines: bfloat16 [20480, 512], P(('outer', 'inner')), may hold values from -8 to 8
- partner: int32 [20480], P('outer'), may hold values from 0 to 20479, each once
- note_days: int32 [20480], P('outer'), may hold values from 0 to 479
- time_days: int32 [20480], P(('outer', 'inner')), may hold values from 0 to 479
- logit_scale: float32 [1], replicated, may hold values from 0.25 to 0.5
- bias: float32 [8], replicated, may hold values from -2 to 2
Outputs:
- mean_loss: float32 [1], replicated
- bias_grad: float32 [8], replicated
- note_grad: float32 [20480, 512], P(('outer', 'inner'))
- time_grad: float32 [20480, 512], P(('outer', 'inner'))
Inputs may be any that keep to these rules, and one draw needn't show every extreme that they name: Each timeline is the partner of exactly one note.
All inputs are finite; a program needn't handle non-finite values.
Results may differ from a plain program's by a relative error of at most 0.00255.
Values may be sent and summed in bfloat16 or wider, within the bound.
A program may use at most 64 MiB of HBM per device.

v0:
```python
import math

import jax
import jax.numpy as jnp
from jax import lax
from jax.sharding import PartitionSpec as P

bucket_days = 30


def combined_all(value, axis, join):
    pieces = jax.tree.map(lambda part: lax.all_gather(part, axis), value)
    head = jax.tree.map(lambda part: part[0], pieces)
    tail = jax.tree.map(lambda part: part[1:], pieces)
    subtotal, _ = lax.scan(lambda subtotal, share: (join(subtotal, share), None), head, tail)
    return subtotal


def pair_logits(note_rows, note_when, time_rows, time_when, scale, bias):
    raw = lax.dot_general(
        note_rows, time_rows, (((1,), (1,)), ((), ())), preferred_element_type=jnp.float32
    )
    bucket = jnp.minimum(
        jnp.abs(note_when[:, None] - time_when[None, :]) // bucket_days, bias.shape[0] - 1
    ).astype(jnp.int32)
    offset = jnp.zeros(raw.shape, jnp.float32)
    for level in range(bias.shape[0]):
        offset = offset + jnp.where(bucket == level, bias[level], 0.0)
    return (raw * scale + offset, bucket)


def combine_stats(first, second):
    peak = jnp.maximum(first[0], second[0])
    return (peak, first[1] * jnp.exp(first[0] - peak) + second[1] * jnp.exp(second[0] - peak))


def body(notes, timelines, partner, note_days, time_days, logit_scale, bias):
    note_count = notes.shape[0]
    own_count = timelines.shape[0]
    scale = logit_scale[0] / math.sqrt(notes.shape[1])
    inner_size = lax.axis_size("inner")
    inner_id = lax.axis_index("inner")
    outer_id = lax.axis_index("outer")
    time_span = own_count * lax.axis_size("outer")

    def global_cols(count):
        position = jnp.arange(count, dtype=jnp.int32)
        return (position // own_count * inner_size + inner_id) * own_count + position % own_count

    start_stats = (
        jnp.full((note_count,), -1e30, jnp.float32),
        jnp.zeros((note_count,), jnp.float32),
        jnp.full((time_span,), -1e30, jnp.float32),
        jnp.zeros((time_span,), jnp.float32),
        jnp.zeros((), jnp.float32),
    )
    time_rows = lax.all_gather(timelines, "outer", axis=0, tiled=True)
    when = lax.all_gather(time_days, "outer", axis=0, tiled=True)
    count = time_rows.shape[0]
    logits, bucket = pair_logits(notes, note_days, time_rows, when, scale, bias)
    peak = jnp.max(logits, axis=1)
    total = jnp.sum(jnp.exp(logits - peak[:, None]), axis=1)
    rows = combine_stats((start_stats[0], start_stats[1]), (peak, total))
    col_peak = jnp.max(logits, axis=0)
    col_total = jnp.sum(jnp.exp(logits - col_peak[None, :]), axis=0)
    peaks = col_peak
    totals = col_total
    positive = jnp.sum(jnp.where(partner[:, None] == global_cols(count)[None, :], logits, 0.0))
    partial_stats = (rows[0], rows[1], peaks, totals, positive)
    time_group = (
        lax.all_gather(timelines, "outer", axis=0, tiled=True),
        lax.all_gather(time_days, "outer", axis=0, tiled=True),
    )
    row_peak, row_total = combined_all((partial_stats[0], partial_stats[1]), "inner", combine_stats)
    col_peak, col_total = combined_all((partial_stats[2], partial_stats[3]), "outer", combine_stats)
    row_logsum = row_peak + jnp.log(row_total)
    col_logsum = col_peak + jnp.log(col_total)
    time_rows, when = time_group
    logits, bucket = pair_logits(notes, note_days, time_rows, when, scale, bias)
    positive = (partner[:, None] == global_cols(time_span)[None, :]).astype(jnp.float32)
    dlogit = (
        0.5 * jnp.exp(logits - row_logsum[:, None])
        + 0.5 * jnp.exp(logits - col_logsum[None, :])
        - positive
    )
    weights = dlogit.astype(jnp.bfloat16)
    note_part = scale * jnp.dot(weights, time_rows, preferred_element_type=jnp.float32)
    bucket_part = jnp.stack(
        [jnp.sum(jnp.where(bucket == level, dlogit, 0.0)) for level in range(bias.shape[0])]
    )
    own_rows = lax.dynamic_slice_in_dim(row_logsum, inner_id * own_count, own_count)
    own_cols = lax.dynamic_slice_in_dim(col_logsum, outer_id * own_count, own_count)
    loss_part = 0.5 * jnp.sum(own_rows) + 0.5 * jnp.sum(own_cols) - partial_stats[4]
    loss_total, bucket_total = lax.psum((loss_part, bucket_part), ("outer", "inner"))
    all_pairs = note_count * lax.axis_size("outer")
    note_grad = lax.psum_scatter(note_part, "inner", scatter_dimension=0, tiled=True)
    time_part = scale * lax.dot_general(
        weights, notes, (((0,), (0,)), ((), ())), preferred_element_type=jnp.float32
    )
    time_grad = lax.psum_scatter(time_part, "outer", scatter_dimension=0, tiled=True)
    return ((loss_total / all_pairs).reshape(1), bucket_total / all_pairs, note_grad, time_grad)


def solution(mesh):
    placed = (
        P("outer", None),
        P(("outer", "inner"), None),
        P("outer"),
        P("outer"),
        P(("outer", "inner")),
        P(),
        P(),
    )
    return jax.shard_map(
        body,
        mesh=mesh,
        in_specs=placed,
        out_specs=(P(), P(), P(("outer", "inner"), None), P(("outer", "inner"), None)),
        check_vma=False,
    )
```

profile of v0, /device:TPU:192, one launch (start us, length us, event | category | flops | bytes accessed | tf_op | source)
XLA Modules:
  0.0 1001.4 jit_solution(16977746415187497659)
XLA Ops:
  7.2 0.7 all-gather.8.cloned.1.call-update
  7.9 0.0 reduce-scatter.3.cloned.1.call-start
  8.6 1.3 dynamic-slice
  10.5 0.9 dynamic-update-slice
  11.4 28.3 %all-reduce = s32[1280]{0:T(1024)S(1)} all-reduce(s32[1280]{0:T(1024)S(1)} %dynamic-update-slice), channel_id=1, replica_groups=mesh['outer'=32,'inner'=16] {'outer'}, use_global_device_ids=true, to_apply=%add | all-reduce | flops 1280 | bytes 10240
  39.8 1.6 fusion.20
  41.4 83.2 %all-gather.8.cloned.1.call-done = bf16[1280,512]{1,0:T(8,128)(2,1)} async-done(((bf16[40,512]{1,0:T(8,128)(2,1)}), bf16[1280,512]{1,0:T(8,128)(2,1)}) %all-gather.8.cloned.1.call-update) | async-done | bytes 1310736 | tf_op jit(solution)/shard_map/all_gather | solution.py:57
  124.6 12.5 %fusion.18 = (f32[1280]{0:T(1024)S(1)}, f32[640]{0:T(1024)S(1)}, f32[640,1280]{1,0:T(8,128)S(1)}) fusion(f32[]{:T(128)} %bitcast.9, f32[]{:T(128)} %bitcast.8, f32[]{:T(128)} %bitcast.7, f32[]{:T(128)} %bitcast.6, f32[]{:T(128)} %bitcast.5, f32[]{:T(128)} %bitcast.4, f32[]{:T(128)} %bitcast.3, f32[]{:T(128)} %bitcast.2, s32[1280]{0:T(1024)S(1)} %all-reduce, ...), kind=kOutput, calls=%fused_computation.70 | convolution fusion | flops 869988480 | bytes 5258276 | tf_op jit(solution)/shard_map/dot_general | solution.py:20
  137.1 155.2 %all-gather.4 = f32[32,1,1280]{2,1,0:T(1,128)S(1)} all-gather(f32[1,1,1280]{2,1,0:T(1,128)S(1)} %reshape.93), channel_id=2, replica_groups=mesh['outer'=32,'inner'=16] {'outer'}, dimensions={0}, use_global_device_ids=true | all-gather | bytes 168960 | tf_op jit(solution)/shard_map/all_gather | solution.py:12
  292.3 2.2 fusion.1
  294.6 148.5 %all-gather.5 = f32[32,1,1280]{2,1,0:T(1,128)S(1)} all-gather(f32[1,1,1280]{2,1,0:T(1,128)S(1)} %reshape.95), channel_id=3, replica_groups=mesh['outer'=32,'inner'=16] {'outer'}, dimensions={0}, use_global_device_ids=true | all-gather | bytes 168960 | tf_op jit(solution)/shard_map/all_gather | solution.py:12
  443.2 24.0 %all-gather.2 = f32[16,1,640]{2,1,0:T(1,128)S(1)} all-gather(f32[1,1,640]{2,1,0:T(1,128)S(1)} %get-tuple-element.109), channel_id=1, replica_groups=mesh['outer'=32,'inner'=16] {'inner'}, dimensions={0}, use_global_device_ids=true | all-gather | bytes 43520 | tf_op jit(solution)/shard_map/all_gather | solution.py:12
  467.2 25.9 %all-gather.3 = f32[16,1,640]{2,1,0:T(1,128)S(1)} all-gather(f32[1,1,640]{2,1,0:T(1,128)S(1)} %get-tuple-element.108), channel_id=1, replica_groups=mesh['outer'=32,'inner'=16] {'inner'}, dimensions={0}, use_global_device_ids=true | all-gather | bytes 43520 | tf_op jit(solution)/shard_map/all_gather | solution.py:12
  493.2 2.6 while.25
  495.8 1.0 while.24
  496.8 8.8 select_reduce_fusion
  505.6 3.4 convolution_multiply_fusion.2
  509.1 0.0 reduce-scatter.5.cloned.1.call-start
  509.1 2.7 convolution_multiply_fusion.1
  511.9 0.8 dynamic-slice_reduce_fusion.4
  514.6 5.0 stack.35
  519.6 104.8 %all-reduce.1 = (f32[]{:T(128)}, f32[8]{0:T(128)S(1)}) all-reduce(f32[]{:T(128)S(6)} %sub.117, f32[8]{0:T(128)S(1)} %stack.35), channel_id=1, replica_groups=mesh['outer'=32,'inner'=16] {'outer','inner'}, use_global_device_ids=true, to_apply=%region_11.12 | all-reduce | flops 9 | bytes 72 | tf_op jit(solution)/shard_map/psum | solution.py:94
  625.0 0.5 broadcast_multiply_fusion
  625.6 368.2 %reduce-scatter.5.cloned.1.call-done = f32[40,512]{1,0:T(8,128)} async-done(((f32[1280,512]{1,0:T(8,128)}), f32[40,512]{1,0:T(8,128)}) %reduce-scatter.5.cloned.1.call-update) | async-done | bytes 81936 | tf_op jit(solution)/shard_map/reduce_scatter | solution.py:100
  (123 shorter events, 2.6 us)
Async XLA Ops:
  7.2 117.4 %copy-start = (bf16[640,512]{1,0:T(8,128)(2,1)S(1)}, bf16[640,512]{1,0:T(8,128)(2,1)}, u32[]{:S(2)}) copy-start(bf16[640,512]{1,0:T(8,128)(2,1)} %param.11) | copy-start | bytes 1966084
  7.2 117.4 %all-gather.8.cloned.1.call-start = ((), (), s32[]{:S(2)}) async-start(), calls=%async_computation.2 | async-start | bytes 1351680 | tf_op jit(solution)/shard_map/all_gather | solution.py:57
  7.9 617.6 %reduce-scatter.3.cloned.1.call-start = ((), (), s32[]{:S(2)}) async-start(), calls=%async_computation.3 | async-start | bytes 1392640 | tf_op jit(solution)/shard_map/reduce_scatter | solution.py:96
  124.6 167.7 %copy-start.2 = (s32[640]{0:T(1024)S(1)}, s32[640]{0:T(1024)}, u32[]{:S(2)}) copy-start(s32[640]{0:T(1024)} %param.13) | copy-start | bytes 7684
  137.0 155.2 %copy-start.1 = (f32[640,1280]{1,0:T(8,128)}, f32[640,1280]{1,0:T(8,128)S(1)}, u32[]{:S(2)}) copy-start(f32[640,1280]{1,0:T(8,128)S(1)} %get-tuple-element.118) | copy-start | bytes 9830404
  137.1 359.8 %copy-start.3 = (s32[640]{0:T(1024)S(1)}, s32[640]{0:T(1024)}, u32[]{:S(2)}) copy-start(s32[640]{0:T(1024)} %param.14) | copy-start | bytes 7684
  509.1 484.7 %reduce-scatter.5.cloned.1.call-start = ((), (), s32[]{:S(2)}) async-start(), calls=%async_computation.4 | async-start | bytes 2703360 | tf_op jit(solution)/shard_map/reduce_scatter | solution.py:100
Sparse Core Ops, SparseCore 0:
  12.3 112.2 all-gather.7
  509.2 91.9 reduce-scatter.2
  604.6 389.0 reduce-scatter.4
where the time goes:
time: 1000 us
  blocking collectives  487 us (49%)
  waiting for transfers between devices  452 us (45%)
  between operations  19 us (2%)
  matrix products  18.6 us (2%)
  other arithmetic  13 us (1%)
  local copies, waits for them, and re-layouts  10.6 us (1%)
    reduce_scatter x1, waiting for transfers between devices, body(): lax.psum_scatter(time_part, 'outer', scatter_dimension=0, tiled=True)  368 us
    all_gather x4, blocking collectives, combined_all(): pieces = jax.tree.map(lambda part: lax.all_gather(part, axis), value)  354 us
    psum x1, blocking collectives, body(): lax.psum((loss_part, bucket_part), ('outer', 'inner'))  105 us
    all_gather x1, waiting for transfers between devices, body(): time_rows = lax.all_gather(timelines, 'outer', axis=0, tiled=True)  83.2 us
    unnamed x1, blocking collectives  28.3 us
  transfers between devices with their start and end apart: 3, of which 2 were waited for; matrix products, arithmetic and copies ran while one was open for 1% of the time, Pallas kernels for 0%

commit v1 on v0

v1 whole, which is shorter than its diff:
```python
import functools
import math

import jax
import jax.numpy as jnp
from jax import lax
from jax.experimental import pallas as pl
from jax.experimental.pallas import tpu as pltpu
from jax.sharding import PartitionSpec as P

BUCKET_DAYS = 30
LOG2E = math.log2(math.e)
LN2 = math.log(2.0)
MESH = pl.DeviceIdType.MESH
F32 = jnp.float32
BF16 = jnp.bfloat16


def log2_sum(parts):
    peak = functools.reduce(jnp.maximum, parts)
    total = functools.reduce(jnp.add, [jnp.exp2(part - peak) for part in parts])
    return peak + jnp.log2(total)


def spread_rows(row, width):
    return jnp.broadcast_to(row, (width, row.shape[1])).T


def kernel(
    sizes,
    scale_ref, bias_ref, notes_ref, time_ref, when_ref, note_when_ref, partner_ref,
    note_grad_ref, time_grad_ref, summary_ref,
    shards, shard_days, stage, planes, logits, weights, when_col, partner_col, row_col, spare,
    row_stats, col_stats, col_far, part, time_out, time_in, far_in,
    note_near, note_out, note_in, note_own, level_sums, inner_sums, plane_sums, far_sums,
    g_send, g_recv, d_send, d_recv, r_send, r_recv, c_send, c_recv, t_send, t_recv,
    n_send, n_recv, m_send, m_recv, a_send, a_recv, b_send, b_recv,
):
    nx, ny, nz = sizes
    nq = nx * ny
    rows, depth = notes_ref.shape
    own = time_ref.shape[0]
    span = nq * own
    step = min(128, rows)
    blocks = rows // step
    wide = when_col.shape[1]
    levels = bias_ref.shape[0]

    outer_id, inner_id = lax.axis_index("outer"), lax.axis_index("inner")
    q, far = outer_id // 2, outer_id % 2
    qx, qy = q // ny, q % ny
    line, core = inner_id // 2, inner_id % 2

    def plane_peer(s):
        return lax.rem(qx + s // ny, nx) * ny + lax.rem(qy + s % ny, ny)

    def in_plane(peer):
        return (peer * 2 + far, inner_id)

    across = (q * 2 + 1 - far, inner_id)

    def inner_peer(s):
        return lax.rem(inner_id + s, 2 * nz)

    def send(src, dst, send_sem, recv_sem, device):
        pltpu.make_async_remote_copy(
            src_ref=src, dst_ref=dst, send_sem=send_sem, recv_sem=recv_sem,
            device_id=device, device_id_type=MESH,
        ).start()

    def wait_in(dst, recv_sem):
        pltpu.make_async_copy(dst, dst, recv_sem).wait()

    wait_out = wait_in

    barrier = pltpu.get_barrier_semaphore()

    def hello_plane(s, _):
        pl.semaphore_signal(barrier, inc=1, device_id=in_plane(plane_peer(s)), device_id_type=MESH)
        return 0

    def hello_inner(s, _):
        pl.semaphore_signal(barrier, inc=1, device_id=(outer_id, inner_peer(s)), device_id_type=MESH)
        return 0

    pl.semaphore_signal(barrier, inc=1, device_id=across, device_id_type=MESH)
    lax.fori_loop(1, nq, hello_plane, 0)
    lax.fori_loop(1, 2 * nz, hello_inner, 0)

    scale = scale_ref[0] * F32(LOG2E / math.sqrt(depth))
    lane = lax.broadcasted_iota(jnp.int32, (1, span), 1)
    lane_q = ((lane.astype(F32) + 0.5) * F32(1.0 / own)).astype(jnp.int32)
    shards[0, q] = time_ref[...]
    shard_days[0, q] = jnp.where(lane_q == q, when_ref[...].astype(F32), 0.0)
    pl.semaphore_wait(barrier, 1 + (nq - 1) + (2 * nz - 1))

    send(time_ref, shards.at[1, q], g_send.at[1, q], g_recv.at[1, q], across)
    send(shard_days.at[0, q], shard_days.at[1, q], d_send.at[1, q], d_recv.at[1, q], across)

    def share(plane):
        def one(s, _):
            peer = plane_peer(s)
            send(shards.at[plane, q], shards.at[plane, q], g_send.at[plane, peer], g_recv.at[plane, q], in_plane(peer))
            send(shard_days.at[plane, q], shard_days.at[plane, q], d_send.at[plane, peer], d_recv.at[plane, q],
                 in_plane(peer))
            return 0
        lax.fori_loop(1, nq, one, 0)

    share(0)
    when_col[...] = spread_rows(note_when_ref[...].astype(F32), wide)
    partner_col[...] = spread_rows(partner_ref[...].astype(F32), wide)
    wait_in(shards.at[1, q], g_recv.at[1, q])
    wait_in(shard_days.at[1, q], d_recv.at[1, q])
    share(1)

    def gap(block, plane, days):
        return jnp.abs(when_col[pl.ds(block * step, step), 0:1] - days)

    def ids(plane):
        zone = far if plane == 0 else 1 - far
        return (((lane_q * 2 + zone) * (2 * nz) + inner_id) * own + (lane - lane_q * own)).astype(F32)

    def plane_days(plane):
        return functools.reduce(jnp.add, [shard_days[plane, k] for k in range(nq)])

    positive = jnp.zeros((8, span), F32)
    col_logs = []
    for plane in range(2):
        def arrive(s, _):
            peer = plane_peer(s)
            wait_in(shards.at[plane, peer], g_recv.at[plane, peer])
            wait_in(shard_days.at[plane, peer], d_recv.at[plane, peer])
            return 0
        lax.fori_loop(1, nq, arrive, 0)

        def settle(k, _):
            stage[pl.ds(pl.multiple_of(k * own, own), own)] = shards[plane, k].astype(F32)
            return 0
        lax.fori_loop(0, nq, settle, 0)
        planes[plane] = stage[...].astype(BF16)
        days = plane_days(plane)
        names = ids(plane)
        cols = pl.ds(plane * span, span)

        def logit_block(block, carry):
            col_peak, positive = carry
            here = pl.ds(pl.multiple_of(block * step, step), step)
            raw = lax.dot_general(notes_ref[here], planes[plane], (((1,), (1,)), ((), ())),
                                  preferred_element_type=F32)
            distance = gap(block, plane, days)
            offset = jnp.full(raw.shape, bias_ref[0] * F32(LOG2E), F32)
            for level in range(1, levels):
                offset = jnp.where(distance >= F32(BUCKET_DAYS * level), bias_ref[level] * F32(LOG2E), offset)
            value = raw * scale + offset
            logits[here, cols] = value
            peak = jnp.max(value, axis=1, keepdims=True)
            total = jnp.sum(jnp.exp2(value - peak), axis=1, keepdims=True)
            spare[plane, here] = jnp.broadcast_to(peak + jnp.log2(total), (step, wide))
            hit = jnp.where(partner_col[here, 0:1] == names, value, 0.0)
            positive = positive + jnp.sum(hit.reshape(step // 8, 8, span), axis=0)
            return (jnp.maximum(col_peak, jnp.max(value, axis=0, keepdims=True)), positive)

        col_peak, positive = lax.fori_loop(
            0, blocks, logit_block, (jnp.full((1, span), -jnp.inf, F32), positive))

        def col_block(block, total):
            here = pl.ds(pl.multiple_of(block * step, step), step)
            return total + jnp.sum(jnp.exp2(logits[here, cols] - col_peak), axis=0, keepdims=True)

        col_total = lax.fori_loop(0, blocks, col_block, jnp.zeros((1, span), F32))
        col_logs.append(col_peak + jnp.log2(col_total))

    row_stats[inner_id] = log2_sum([spare[0], spare[1]]).T[0:1]

    def share_rows(s, _):
        peer = inner_peer(s)
        send(row_stats.at[inner_id], row_stats.at[inner_id], r_send.at[peer], r_recv.at[inner_id], (outer_id, peer))
        return 0

    for plane in range(2):
        col_stats[q, 0:1, pl.ds(plane * span, span)] = col_logs[plane]

    def share_cols(s, _):
        peer = plane_peer(s)
        send(col_stats.at[q], col_stats.at[q], c_send.at[peer], c_recv.at[q], in_plane(peer))
        return 0

    lax.fori_loop(1, nq, share_cols, 0)
    lax.fori_loop(1, 2 * nz, share_rows, 0)

    def cols_in(s, _):
        peer = plane_peer(s)
        wait_in(col_stats.at[peer], c_recv.at[peer])
        return 0

    lax.fori_loop(1, nq, cols_in, 0)
    near = log2_sum([col_stats[k] for k in range(nq)])
    col_far[0] = near
    send(col_far.at[0], col_far.at[1], c_send.at[q], c_recv.at[q], across)

    def rows_in(s, _):
        peer = inner_peer(s)
        wait_in(row_stats.at[peer], r_recv.at[peer])
        return 0

    lax.fori_loop(1, 2 * nz, rows_in, 0)
    row_log = log2_sum([row_stats[k] for k in range(2 * nz)])
    row_col[...] = spread_rows(row_log + 1.0, wide)
    wait_in(col_far.at[1], c_recv.at[q])
    there = col_far[1]
    col_log = [
        log2_sum([near[:, :span], there[:, span:]]),
        log2_sum([near[:, span:], there[:, :span]]),
    ]

    for plane in (1, 0):
        cols = pl.ds(plane * span, span)
        names = ids(plane)
        col_half = col_log[plane] + 1.0

        def weight_block(block, _):
            here = pl.ds(pl.multiple_of(block * step, step), step)
            value = logits[here, cols]
            value = (
                jnp.exp2(value - row_col[here, 0:1])
                + jnp.exp2(value - col_half)
                - jnp.where(partner_col[here, 0:1] == names, 1.0, 0.0)
            )
            logits[here, cols] = value
            weights[here, cols] = value.astype(BF16)
            return 0

        lax.fori_loop(0, blocks, weight_block, 0)

        wide_step = min(128, span)

        def time_block(block, _):
            here = pl.ds(pl.multiple_of(block * wide_step, wide_step), wide_step)
            from_here = pl.ds(pl.multiple_of(plane * span + block * wide_step, wide_step), wide_step)
            stage[here] = lax.dot_general(weights[:, from_here], notes_ref[...], (((0,), (0,)), ((), ())),
                                          preferred_element_type=F32)
            return 0

        lax.fori_loop(0, span // wide_step, time_block, 0)

        def share_time(s, _):
            peer = plane_peer(s)
            time_out[plane, peer] = stage[pl.ds(pl.multiple_of(peer * own, own), own)].astype(BF16)
            send(time_out.at[plane, peer], time_in.at[plane, q], t_send.at[plane, peer], t_recv.at[plane, q],
                 in_plane(peer))
            return 0

        lax.fori_loop(1, nq, share_time, 0)
        part[plane] = stage[pl.ds(pl.multiple_of(q * own, own), own)]

    def note_block(block, _):
        here = pl.ds(pl.multiple_of(block * step, step), step)
        stage_rows = jnp.dot(weights[here, 0:span], planes[0], preferred_element_type=F32)
        note_own[here] = stage_rows + jnp.dot(weights[here, span:2 * span], planes[1], preferred_element_type=F32)
        return 0

    lax.fori_loop(0, blocks, note_block, 0)

    def share_core(k, _):
        there = pl.ds(pl.multiple_of((2 * k + 1 - core) * own, own), own)
        send(note_own.at[there], note_near.at[k], n_send.at[k], n_recv.at[k], (outer_id, 2 * line + 1 - core))
        return 0

    lax.fori_loop(0, nz, share_core, 0)

    level_sums[...] = jnp.zeros_like(level_sums)
    for plane in range(2):
        days = plane_days(plane)
        cols = pl.ds(plane * span, span)

        def level_block(block, _):
            here = pl.ds(pl.multiple_of(block * step, step), step)
            value = logits[here, cols]
            distance = gap(block, plane, days)
            for level in range(levels):
                picked = value if level == 0 else jnp.where(distance >= F32(BUCKET_DAYS * level), value, 0.0)
                level_sums[level] += jnp.sum(picked.reshape(step // 8, 8, span), axis=0)
            return 0

        if plane == 0:
            lax.fori_loop(0, blocks, level_block, 0)

            def share_line(s, _):
                k = lax.rem(line + s, nz)
                wait_in(note_near.at[k], n_recv.at[k])
                mine = pl.ds(pl.multiple_of((2 * k + core) * own, own), own)
                note_out[k] = (note_own[mine] + note_near[k]).astype(BF16)
                send(note_out.at[k], note_in.at[line], m_send.at[k], m_recv.at[line], (outer_id, 2 * k + core))
                return 0

            lax.fori_loop(1, nz, share_line, 0)
        else:
            lax.fori_loop(0, blocks, level_block, 0)

    above = jnp.sum(jnp.sum(level_sums[...], axis=1), axis=1, keepdims=True)
    below = jnp.concatenate([above[1:], jnp.zeros((1, 1), F32)], axis=0)
    loss = F32(LN2) * (
        (0.5 / (2 * nz)) * jnp.sum(row_log)
        + (0.5 / (2 * nq)) * (jnp.sum(col_log[0]) + jnp.sum(col_log[1]))
        - jnp.sum(positive)
    )
    column = lax.broadcasted_iota(jnp.int32, (levels, wide), 1)
    inner_sums[inner_id] = jnp.where(column == 0, above - below, jnp.where(column == 1, loss, 0.0))

    def share_sums(s, _):
        peer = inner_peer(s)
        send(inner_sums.at[inner_id], inner_sums.at[inner_id], a_send.at[peer], a_recv.at[inner_id], (outer_id, peer))
        return 0

    lax.fori_loop(1, 2 * nz, share_sums, 0)

    def time_arrive(plane):
        def one(s, _):
            peer = plane_peer(s)
            wait_in(time_in.at[plane, peer], t_recv.at[plane, peer])
            part[plane] += time_in[plane, peer].astype(F32)
            return 0
        lax.fori_loop(1, nq, one, 0)

    time_arrive(1)
    send(part.at[1], far_in, t_send.at[1, q], t_recv.at[1, q], across)

    def sums_in(s, _):
        peer = inner_peer(s)
        wait_in(inner_sums.at[peer], a_recv.at[peer])
        return 0

    lax.fori_loop(1, 2 * nz, sums_in, 0)
    plane_sums[q] = functools.reduce(jnp.add, [inner_sums[k] for k in range(2 * nz)])

    def share_plane_sums(s, _):
        peer = plane_peer(s)
        send(plane_sums.at[q], plane_sums.at[q], b_send.at[peer], b_recv.at[q], in_plane(peer))
        return 0

    lax.fori_loop(1, nq, share_plane_sums, 0)
    time_arrive(0)

    def plane_sums_in(s, _):
        peer = plane_peer(s)
        wait_in(plane_sums.at[peer], b_recv.at[peer])
        return 0

    lax.fori_loop(1, nq, plane_sums_in, 0)
    far_sums[0] = functools.reduce(jnp.add, [plane_sums[k] for k in range(nq)])
    send(far_sums.at[0], far_sums.at[1], b_send.at[q], b_recv.at[q], across)

    factor = scale_ref[0] * F32(1.0 / math.sqrt(depth))
    wait_in(note_near.at[line], n_recv.at[line])
    total = note_own[pl.ds(pl.multiple_of((2 * line + core) * own, own), own)] + note_near[line]
    spare_total = total

    def note_arrive(s, total):
        k = lax.rem(line + s, nz)
        wait_in(note_in.at[k], m_recv.at[k])
        return total + note_in[k].astype(F32)

    note_grad_ref[...] = factor * lax.fori_loop(1, nz, note_arrive, spare_total)
    wait_in(far_in, t_recv.at[1, q])
    time_grad_ref[...] = factor * (part[0] + far_in[...])
    wait_in(far_sums.at[1], b_recv.at[q])
    summary_ref[...] = (far_sums[0] + far_sums[1]) * F32(1.0 / (rows * 2 * nq))

    wait_out(time_ref, g_send.at[1, q])
    wait_out(shard_days.at[0, q], d_send.at[1, q])
    wait_out(col_far.at[0], c_send.at[q])
    wait_out(part.at[1], t_send.at[1, q])
    wait_out(far_sums.at[0], b_send.at[q])

    def plane_left(s, _):
        peer = plane_peer(s)
        for plane in range(2):
            wait_out(shards.at[plane, q], g_send.at[plane, peer])
            wait_out(shard_days.at[plane, q], d_send.at[plane, peer])
            wait_out(time_out.at[plane, peer], t_send.at[plane, peer])
        wait_out(col_stats.at[q], c_send.at[peer])
        wait_out(plane_sums.at[q], b_send.at[peer])
        return 0

    def inner_left(s, _):
        peer = inner_peer(s)
        wait_out(row_stats.at[inner_id], r_send.at[peer])
        wait_out(inner_sums.at[inner_id], a_send.at[peer])
        return 0

    def core_left(k, _):
        there = pl.ds(pl.multiple_of((2 * k + 1 - core) * own, own), own)
        wait_out(note_own.at[there], n_send.at[k])
        return 0

    def line_left(s, _):
        k = lax.rem(line + s, nz)
        wait_out(note_out.at[k], m_send.at[k])
        return 0

    lax.fori_loop(1, nq, plane_left, 0)
    lax.fori_loop(1, 2 * nz, inner_left, 0)
    lax.fori_loop(0, nz, core_left, 0)
    lax.fori_loop(1, nz, line_left, 0)


def body(notes, timelines, partner, note_days, time_days, logit_scale, bias):
    rows, depth = notes.shape
    own = timelines.shape[0]
    nq = lax.axis_size("outer") // 2
    nz = lax.axis_size("inner") // 2
    ny = 2 ** (int(math.log2(nq)) // 2)
    span = nq * own
    levels = bias.shape[0]
    wide = 128
    vmem, smem = pl.BlockSpec(memory_space=pltpu.VMEM), pl.BlockSpec(memory_space=pltpu.SMEM)
    dma = pltpu.SemaphoreType.DMA
    note_grad, time_grad, summary = pl.pallas_call(
        functools.partial(kernel, (nq // ny, ny, nz)),
        out_shape=(
            jax.ShapeDtypeStruct((own, depth), F32),
            jax.ShapeDtypeStruct((own, depth), F32),
            jax.ShapeDtypeStruct((levels, wide), F32),
        ),
        in_specs=[smem, smem] + [vmem] * 5,
        out_specs=(vmem,) * 3,
        scratch_shapes=[
            pltpu.VMEM((2, nq, own, depth), BF16),
            pltpu.VMEM((2, nq, 1, span), F32),
            pltpu.VMEM((span, depth), F32),
            pltpu.VMEM((2, span, depth), BF16),
            pltpu.VMEM((rows, 2 * span), F32),
            pltpu.VMEM((rows, 2 * span), BF16),
            pltpu.VMEM((rows, wide), F32),
            pltpu.VMEM((rows, wide), F32),
            pltpu.VMEM((rows, wide), F32),
            pltpu.VMEM((2, rows, wide), F32),
            pltpu.VMEM((2 * nz, 1, rows), F32),
            pltpu.VMEM((nq, 1, 2 * span), F32),
            pltpu.VMEM((2, 1, 2 * span), F32),
            pltpu.VMEM((2, own, depth), F32),
            pltpu.VMEM((2, nq, own, depth), BF16),
            pltpu.VMEM((2, nq, own, depth), BF16),
            pltpu.VMEM((own, depth), F32),
            pltpu.VMEM((nz, own, depth), F32),
            pltpu.VMEM((nz, own, depth), BF16),
            pltpu.VMEM((nz, own, depth), BF16),
            pltpu.VMEM((rows, depth), F32),
            pltpu.VMEM((levels, 8, span), F32),
            pltpu.VMEM((2 * nz, levels, wide), F32),
            pltpu.VMEM((nq, levels, wide), F32),
            pltpu.VMEM((2, levels, wide), F32),
            dma((2, nq)), dma((2, nq)), dma((2, nq)), dma((2, nq)),
            dma((2 * nz,)), dma((2 * nz,)), dma((nq,)), dma((nq,)),
            dma((2, nq)), dma((2, nq)),
            dma((nz,)), dma((nz,)), dma((nz,)), dma((nz,)),
            dma((2 * nz,)), dma((2 * nz,)), dma((nq,)), dma((nq,)),
        ],
        compiler_params=pltpu.CompilerParams(
            collective_id=0, has_side_effects=True, vmem_limit_bytes=48 * 2**20
        ),
    )(
        logit_scale, bias, notes, timelines,
        jnp.tile(time_days, nq).reshape(1, span),
        note_days.reshape(1, rows),
        partner.reshape(1, rows),
    )
    return (summary[0, 1:2], summary[:, 0], note_grad, time_grad)


def solution(mesh):
    placed = (
        P("outer", None),
        P(("outer", "inner"), None),
        P("outer"),
        P("outer"),
        P(("outer", "inner")),
        P(),
        P(),
    )
    return jax.shard_map(
        body,
        mesh=mesh,
        in_specs=placed,
        out_specs=(P(), P(), P(("outer", "inner"), None), P(("outer", "inner"), None)),
        check_vma=False,
    )
```

time: 1000 us -> 111 us (0.11)
  the two profiles are of different devices: /device:TPU:192 before, /device:TPU:1 now
where the time goes in v1:
time: 111 us
  Pallas kernels  103 us (93%)
  local copies, waits for them, and re-layouts  6.37 us (6%)
  between operations  1.33 us (1%)
    pallas_call x1, Pallas kernels, body(): pl.pallas_call(functools.partial(kernel, (nq // ny, ny, nz)), out_shape=(...  103 us
    unnamed x12, local copies, waits for them, and re-layouts  4.41 us

profile of v1, /device:TPU:1, one launch (start us, length us, event | category | flops | bytes accessed | tf_op | source)
XLA Modules:
  0.0 110.7 jit_solution(6194459870996663944)
XLA Ops:
  0.6 0.7 tile.2
  1.3 0.0 copy-start.3
  1.3 0.1 reshape_tile.3.when_ref
  1.4 0.6 copy-done.3
  2.0 0.0 copy-start.4
  2.0 0.7 copy-done.4
  2.7 0.0 copy-start.2
  3.3 0.0 copy-done.2
  3.3 0.0 copy-start
  3.4 1.1 copy-done
  4.4 0.0 copy-start.1
  4.4 0.8 copy-done.1
  5.2 103.0 %shard_map.102 = (f32[40,512]{1,0:T(8,128)S(1)}, f32[40,512]{1,0:T(8,128)S(1)}, f32[8,128]{1,0:T(8,128)S(1)}) custom-call(f32[1]{0:T(128)S(6)} %copy.13.scale_ref, f32[8]{0:T(128)S(1)} %copy-done.2, bf16[640,512]{1,0:T(8,128)(2,1)S(1)} %copy-done, bf16[40,512]{1,0:T(8,128)(2,1)S(1)} %copy-done.1, s32[1,640]{1,0:T(1,128)S(1)} %reshape_tile.3.when_ref, ...), custom_call_target="tpu_custom_call" | custom-call | tf_op jit(solution)/shard_map/pallas_call | solution.py:418
  108.2 0.6 slice.6
  108.8 0.6 slice_reduce_fusion
  109.5 0.6 copy.14
  110.1 0.6 copy.15
  (2 shorter events, 0.0 us)
Async XLA Ops:
  1.3 0.7 copy-start.3
  2.0 0.7 copy-start.4
  2.7 0.7 copy-start.2
  3.3 1.1 copy-start
  4.4 0.8 copy-start.1

commit v2 on v0

v2 whole, which is shorter than its diff:
```python
import functools
import math

import jax
import jax.numpy as jnp
from jax import lax
from jax.experimental import pallas as pl
from jax.experimental.pallas import tpu as pltpu
from jax.sharding import PartitionSpec as P

BUCKET_DAYS = 30
LOG2E = math.log2(math.e)
LN2 = math.log(2.0)
MESH = pl.DeviceIdType.MESH
F32 = jnp.float32
BF16 = jnp.bfloat16


def log2_sum(parts):
    peak = functools.reduce(jnp.maximum, parts)
    total = functools.reduce(jnp.add, [jnp.exp2(part - peak) for part in parts])
    return peak + jnp.log2(total)


def spread_rows(row, width):
    return jnp.broadcast_to(row, (width, row.shape[1])).T


def kernel(
    sizes,
    scale_any, bias_any, notes_any, time_any, when_any, note_when_any, partner_any,
    note_grad_ref, time_grad_ref, summary_ref,
    scale_ref, bias_ref, notes_ref, note_when_ref, partner_ref,
    shards, shard_days, stage, planes, logits, raws, weights, when_col, partner_col, row_col, spare,
    row_stats, col_stats, col_far, part, time_out, time_in, far_out, far_in,
    note_near, note_out, note_in, note_own, level_sums, ring_sums, plane_sums,
    l_sem, g_send, g_recv, d_send, d_recv, r_send, r_recv, c_send, c_recv, f_send, f_recv, t_send, t_recv,
    n_send, n_recv, m_send, m_recv, a_send, a_recv, b_send, b_recv,
):
    nx, ny, nz = sizes
    nq, group = nx * ny, 2 * nz
    rows, depth = notes_ref.shape
    own = time_any.shape[0]
    span = nq * own
    step = min(128, rows)
    blocks = rows // step
    wide = when_col.shape[1]
    levels = bias_ref.shape[0]

    outer_id, inner_id = lax.axis_index("outer"), lax.axis_index("inner")
    q, far = outer_id // 2, outer_id % 2
    qx, qy = q // ny, q % ny
    line, core = inner_id // 2, inner_id % 2
    ring_id = far * group + inner_id

    def plane_peer(s):
        return lax.rem(qx + s // ny, nx) * ny + lax.rem(qy + s % ny, ny)

    def in_plane(peer):
        return (peer * 2 + far, inner_id)

    across = (q * 2 + 1 - far, inner_id)

    def inner_peer(s):
        return lax.rem(inner_id + s, group)

    def ring_peer(s):
        return lax.rem(ring_id + s, 2 * group)

    def on_ring(peer):
        return (q * 2 + peer // group, peer % group)

    def send(src, dst, send_sem, recv_sem, device):
        pltpu.make_async_remote_copy(
            src_ref=src, dst_ref=dst, send_sem=send_sem, recv_sem=recv_sem,
            device_id=device, device_id_type=MESH,
        ).start()

    def wait_in(dst, recv_sem):
        pltpu.make_async_copy(dst, dst, recv_sem).wait()

    wait_out = wait_in

    def each(count, one):
        def run(s, _):
            one(s)
            return 0
        lax.fori_loop(1, count, run, 0)

    barrier = pltpu.get_barrier_semaphore()

    def hello(device):
        pl.semaphore_signal(barrier, inc=1, device_id=device, device_id_type=MESH)

    each(nq, lambda s: hello(in_plane(plane_peer(s))))
    each(2 * group, lambda s: hello(on_ring(ring_peer(s))))

    loads = [
        pltpu.make_async_copy(src, dst, l_sem.at[k])
        for k, (src, dst) in enumerate((
            (time_any, shards.at[0, q]), (when_any, shard_days.at[0, q]), (scale_any, scale_ref), (bias_any, bias_ref),
            (note_when_any, note_when_ref), (partner_any, partner_ref), (notes_any, notes_ref),
        ))
    ]
    for load in loads:
        load.start()
    for load in loads:
        load.wait()
    pl.semaphore_wait(barrier, (nq - 1) + (2 * group - 1))

    send(shards.at[0, q], shards.at[1, q], g_send.at[1, q], g_recv.at[1, q], across)
    send(shard_days.at[0, q], shard_days.at[1, q], d_send.at[1, q], d_recv.at[1, q], across)

    def share(plane):
        def one(s):
            peer = plane_peer(s)
            send(shard_days.at[plane, q], shard_days.at[plane, q], d_send.at[plane, peer], d_recv.at[plane, q],
                 in_plane(peer))
            send(shards.at[plane, q], shards.at[plane, q], g_send.at[plane, peer], g_recv.at[plane, q], in_plane(peer))
        each(nq, one)

    share(0)
    scale = scale_ref[...] * F32(LOG2E / math.sqrt(depth))
    lane = lax.broadcasted_iota(jnp.int32, (1, span), 1)
    lane_q = ((lane.astype(F32) + 0.5) * F32(1.0 / own)).astype(jnp.int32)
    lane_r = lane - lane_q * own
    when_col[...] = spread_rows(note_when_ref[...].reshape(1, rows).astype(F32), wide)
    partner_col[...] = spread_rows(partner_ref[...].reshape(1, rows).astype(F32), wide)
    place = jnp.where(lax.broadcasted_iota(jnp.int32, (own, span), 0) == lane_r, 1.0, 0.0).astype(BF16)

    def plane_days(plane):
        days = jnp.concatenate([shard_days[plane, k] for k in range(nq)], axis=0).astype(F32)
        high = jnp.floor(days * F32(1.0 / 16.0))
        low = days - high * 16.0
        placed = 16.0 * jnp.dot(high.astype(BF16), place, preferred_element_type=F32) + jnp.dot(
            low.astype(BF16), place, preferred_element_type=F32)
        mine = lax.broadcasted_iota(jnp.int32, (nq, span), 0) == lane_q
        return jnp.sum(jnp.where(mine, placed, 0.0), axis=0, keepdims=True)

    def gap(here, days):
        return jnp.abs(when_col[here, 0:1] - days)

    def ids(plane):
        zone = far if plane == 0 else 1 - far
        return (((lane_q * 2 + zone) * group + inner_id) * own + lane_r).astype(F32)

    def by_rows(one, start):
        def run(block, carry):
            return one(pl.ds(pl.multiple_of(block * step, step), step), carry)
        return lax.fori_loop(0, blocks, run, start)

    def cols_of(plane):
        return pl.ds(plane * span, span)

    def days_in(plane):
        def one(s):
            peer = plane_peer(s)
            wait_in(shard_days.at[plane, peer], d_recv.at[plane, peer])
        each(nq, one)
        days = plane_days(plane)

        def offset_block(here, _):
            distance = gap(here, days)
            offset = jnp.full((step, span), bias_ref[0] * F32(LOG2E), F32)
            for level in range(1, levels):
                offset = jnp.where(distance >= F32(BUCKET_DAYS * level), bias_ref[level] * F32(LOG2E), offset)
            logits[here, cols_of(plane)] = offset
            return 0

        by_rows(offset_block, 0)
        return days

    def plane_in(plane):
        def one(s):
            peer = plane_peer(s)
            wait_in(shards.at[plane, peer], g_recv.at[plane, peer])
        each(nq, one)

        def settle(k, _):
            stage[pl.ds(pl.multiple_of(k * own, own), own)] = shards[plane, k].astype(F32)
            return 0
        lax.fori_loop(0, nq, settle, 0)
        planes[plane] = stage[...].astype(BF16)
        cols = cols_of(plane)

        raws[...] = lax.dot_general(notes_ref[...], planes[plane], (((1,), (1,)), ((), ())),
                                    preferred_element_type=F32)

        def logit_block(here, col_peak):
            value = raws[here] * scale + logits[here, cols]
            logits[here, cols] = value
            peak = jnp.max(value, axis=1, keepdims=True)
            total = jnp.sum(jnp.exp2(value - peak), axis=1, keepdims=True)
            spare[plane, here] = jnp.broadcast_to(peak + jnp.log2(total), (step, wide))
            return jnp.maximum(col_peak, jnp.max(value, axis=0, keepdims=True))

        col_peak = by_rows(logit_block, jnp.full((1, span), -jnp.inf, F32))

        def col_block(here, total):
            return total + jnp.sum(jnp.exp2(logits[here, cols] - col_peak), axis=0, keepdims=True)

        col_stats[plane, q] = col_peak + jnp.log2(by_rows(col_block, jnp.zeros((1, span), F32)))

        def share_cols(s):
            peer = plane_peer(s)
            send(col_stats.at[plane, q], col_stats.at[plane, q], c_send.at[plane, peer], c_recv.at[plane, q],
                 in_plane(peer))
        each(nq, share_cols)

    def cols_in(plane):
        def one(s):
            peer = plane_peer(s)
            wait_in(col_stats.at[plane, peer], c_recv.at[plane, peer])
        each(nq, one)
        near = log2_sum([col_stats[plane, k] for k in range(nq)])
        col_far[plane] = near
        send(col_far.at[plane], col_far.at[2 + 1 - plane], f_send.at[plane], f_recv.at[1 - plane], across)
        return near

    def cols_done(plane, near):
        wait_in(col_far.at[2 + plane], f_recv.at[plane])
        return log2_sum([near, col_far[2 + plane]])

    near_days = days_in(0)
    wait_in(shards.at[1, q], g_recv.at[1, q])
    wait_in(shard_days.at[1, q], d_recv.at[1, q])
    share(1)
    plane_in(0)
    far_days = days_in(1)
    near_cols = cols_in(0)
    plane_in(1)

    row_stats[inner_id] = log2_sum([spare[0], spare[1]]).T[0:1]

    def share_rows(s):
        peer = inner_peer(s)
        send(row_stats.at[inner_id], row_stats.at[inner_id], r_send.at[peer], r_recv.at[inner_id], (outer_id, peer))

    each(group, share_rows)
    far_cols = cols_in(1)

    def rows_in(s):
        peer = inner_peer(s)
        wait_in(row_stats.at[peer], r_recv.at[peer])

    each(group, rows_in)
    row_log = log2_sum([row_stats[k] for k in range(group)])
    row_col[...] = spread_rows(row_log + 1.0, wide)
    level_sums[...] = jnp.zeros_like(level_sums)

    def weigh(plane, col_log, positive):
        cols = cols_of(plane)
        names = ids(plane)
        col_half = col_log + 1.0

        def weight_block(here, positive):
            value = logits[here, cols]
            hit = partner_col[here, 0:1] == names
            slope = (
                jnp.exp2(value - row_col[here, 0:1]) + jnp.exp2(value - col_half) - jnp.where(hit, 1.0, 0.0)
            )
            logits[here, cols] = slope
            weights[here, cols] = slope.astype(BF16)
            return positive + jnp.sum(jnp.where(hit, value, 0.0).reshape(step // 8, 8, span), axis=0)

        return by_rows(weight_block, positive)

    def time_partials(plane):
        stage[...] = lax.dot_general(weights[:, plane * span:(plane + 1) * span], notes_ref[...],
                                     (((0,), (0,)), ((), ())), preferred_element_type=F32)

        def share_time(s):
            peer = plane_peer(s)
            time_out[plane, peer] = stage[pl.ds(pl.multiple_of(peer * own, own), own)].astype(BF16)
            send(time_out.at[plane, peer], time_in.at[plane, q], t_send.at[plane, peer], t_recv.at[plane, q],
                 in_plane(peer))

        each(nq, share_time)
        part[plane] = stage[pl.ds(pl.multiple_of(q * own, own), own)]

    def add_levels(plane, days):
        cols = cols_of(plane)

        def level_block(here, _):
            value = logits[here, cols]
            distance = gap(here, days)
            for level in range(levels):
                picked = value if level == 0 else jnp.where(distance >= F32(BUCKET_DAYS * level), value, 0.0)
                level_sums[level] += jnp.sum(picked.reshape(step // 8, 8, span), axis=0)
            return 0

        by_rows(level_block, 0)

    far_log = cols_done(1, far_cols)
    positive = weigh(1, far_log, jnp.zeros((8, span), F32))
    time_partials(1)
    note_own[...] = jnp.dot(weights[:, span:2 * span], planes[1], preferred_element_type=F32)
    add_levels(1, far_days)
    near_log = cols_done(0, near_cols)
    positive = weigh(0, near_log, positive)

    note_own[...] += jnp.dot(weights[:, 0:span], planes[0], preferred_element_type=F32)

    def chunk(k, which):
        return pl.ds(pl.multiple_of((2 * k + which) * own, own), own)

    def share_core(s):
        k = lax.rem(line + s, nz)
        send(note_own.at[chunk(k, 1 - core)], note_near.at[k], n_send.at[k], n_recv.at[k],
             (outer_id, 2 * line + 1 - core))

    each(nz + 1, share_core)
    add_levels(0, near_days)

    above = jnp.sum(level_sums[...], axis=1)
    below = jnp.concatenate([above[1:], jnp.zeros((1, span), F32)], axis=0)
    loss = F32(LN2) * (
        (0.5 / group) * jnp.sum(row_log)
        + (0.5 / (2 * nq)) * (jnp.sum(near_log) + jnp.sum(far_log))
        - jnp.sum(positive)
    )
    buckets = jnp.sum(above - below, axis=1, keepdims=True)
    across_lanes = jnp.where(
        lax.broadcasted_iota(jnp.int32, (levels, wide), 0) == lax.broadcasted_iota(jnp.int32, (levels, wide), 1),
        buckets, 0.0)
    at_loss = lax.broadcasted_iota(jnp.int32, (1, wide), 1) == levels
    ring_sums[ring_id] = jnp.sum(across_lanes, axis=0, keepdims=True) + jnp.where(at_loss, loss, 0.0)

    def share_sums(s):
        peer = ring_peer(s)
        send(ring_sums.at[ring_id], ring_sums.at[ring_id], a_send.at[peer], a_recv.at[ring_id], on_ring(peer))

    each(2 * group, share_sums)

    def share_line(s):
        k = lax.rem(line + s, nz)
        wait_in(note_near.at[k], n_recv.at[k])
        note_out[k] = (note_own[chunk(k, core)] + note_near[k]).astype(BF16)
        send(note_out.at[k], note_in.at[line], m_send.at[k], m_recv.at[line], (outer_id, 2 * k + core))

    each(nz, share_line)
    time_partials(0)

    def time_arrive(plane):
        def one(s):
            peer = plane_peer(s)
            wait_in(time_in.at[plane, peer], t_recv.at[plane, peer])
            part[plane] += time_in[plane, peer].astype(F32)
        each(nq, one)

    time_arrive(1)
    far_out[...] = part[1].astype(BF16)
    send(far_out, far_in, t_send.at[1, q], t_recv.at[1, q], across)

    def sums_in(s):
        peer = ring_peer(s)
        wait_in(ring_sums.at[peer], a_recv.at[peer])

    each(2 * group, sums_in)
    plane_sums[q] = functools.reduce(jnp.add, [ring_sums[k] for k in range(2 * group)])

    def share_plane_sums(s):
        peer = plane_peer(s)
        send(plane_sums.at[q], plane_sums.at[q], b_send.at[peer], b_recv.at[q], in_plane(peer))

    each(nq, share_plane_sums)
    time_arrive(0)

    factor = scale_ref[...] * F32(1.0 / math.sqrt(depth))
    wait_in(note_near.at[line], n_recv.at[line])
    note_near[line] += note_own[chunk(line, core)]

    def note_arrive(s):
        k = lax.rem(line + s, nz)
        wait_in(note_in.at[k], m_recv.at[k])
        note_near[line] += note_in[k].astype(F32)

    each(nz, note_arrive)
    note_grad_ref[...] = factor * note_near[line]

    def plane_sums_in(s):
        peer = plane_peer(s)
        wait_in(plane_sums.at[peer], b_recv.at[peer])

    each(nq, plane_sums_in)
    summary_ref[...] = functools.reduce(jnp.add, [plane_sums[k] for k in range(nq)]) * F32(1.0 / (rows * 2 * nq))
    wait_in(far_in, t_recv.at[1, q])
    time_grad_ref[...] = factor * (part[0] + far_in[...].astype(F32))

    wait_out(shards.at[0, q], g_send.at[1, q])
    wait_out(shard_days.at[0, q], d_send.at[1, q])
    wait_out(far_out, t_send.at[1, q])

    def plane_left(s):
        peer = plane_peer(s)
        for plane in range(2):
            wait_out(shards.at[plane, q], g_send.at[plane, peer])
            wait_out(shard_days.at[plane, q], d_send.at[plane, peer])
            wait_out(col_stats.at[plane, q], c_send.at[plane, peer])
            wait_out(time_out.at[plane, peer], t_send.at[plane, peer])
        wait_out(plane_sums.at[q], b_send.at[peer])

    def line_left(s):
        k = lax.rem(line + s, nz)
        wait_out(note_out.at[k], m_send.at[k])

    for plane in range(2):
        wait_out(col_far.at[plane], f_send.at[plane])
    each(nq, plane_left)
    each(group, lambda s: wait_out(row_stats.at[inner_id], r_send.at[inner_peer(s)]))
    each(2 * group, lambda s: wait_out(ring_sums.at[ring_id], a_send.at[ring_peer(s)]))
    each(nz + 1, lambda s: wait_out(note_near.at[0], n_send.at[lax.rem(line + s, nz)]))
    each(nz, line_left)


def hand_over(note_ref, time_ref, summary_ref, loss_ref, bias_ref, note_out, time_out):
    levels = bias_ref.shape[0]
    note_out[...] = note_ref[...]
    time_out[...] = time_ref[...]
    bias_ref[...] = summary_ref[0, 0:levels]
    loss_ref[...] = summary_ref[0, levels:levels + 1]


def body(notes, timelines, partner, note_days, time_days, logit_scale, bias):
    rows, depth = notes.shape
    own = timelines.shape[0]
    nq = lax.axis_size("outer") // 2
    nz = lax.axis_size("inner") // 2
    ny = 2 ** (int(math.log2(nq)) // 2)
    span = nq * own
    group = 2 * nz
    levels = bias.shape[0]
    wide = 128
    vmem, anywhere = pl.BlockSpec(memory_space=pltpu.VMEM), pl.BlockSpec(memory_space=pltpu.HBM)
    dma = pltpu.SemaphoreType.DMA
    grads = jax.ShapeDtypeStruct((own, depth), F32)
    note_grad, time_grad, summary = pl.pallas_call(
        functools.partial(kernel, (nq // ny, ny, nz)),
        out_shape=(grads, grads, jax.ShapeDtypeStruct((1, wide), F32)),
        in_specs=[anywhere] * 7,
        out_specs=(vmem,) * 3,
        scratch_shapes=[
            pltpu.VMEM((1, 1), F32),
            pltpu.SMEM((levels,), F32),
            pltpu.VMEM((rows, depth), BF16),
            pltpu.VMEM((rows,), jnp.int32),
            pltpu.VMEM((rows,), jnp.int32),
            pltpu.VMEM((2, nq, own, depth), BF16),
            pltpu.VMEM((2, nq, 1, own), jnp.int32),
            pltpu.VMEM((span, depth), F32),
            pltpu.VMEM((2, span, depth), BF16),
            pltpu.VMEM((rows, 2 * span), F32),
            pltpu.VMEM((rows, span), F32),
            pltpu.VMEM((rows, 2 * span), BF16),
            pltpu.VMEM((rows, wide), F32),
            pltpu.VMEM((rows, wide), F32),
            pltpu.VMEM((rows, wide), F32),
            pltpu.VMEM((2, rows, wide), F32),
            pltpu.VMEM((group, 1, rows), F32),
            pltpu.VMEM((2, nq, 1, span), F32),
            pltpu.VMEM((4, 1, span), F32),
            pltpu.VMEM((2, own, depth), F32),
            pltpu.VMEM((2, nq, own, depth), BF16),
            pltpu.VMEM((2, nq, own, depth), BF16),
            pltpu.VMEM((own, depth), BF16),
            pltpu.VMEM((own, depth), BF16),
            pltpu.VMEM((nz, own, depth), F32),
            pltpu.VMEM((nz, own, depth), BF16),
            pltpu.VMEM((nz, own, depth), BF16),
            pltpu.VMEM((rows, depth), F32),
            pltpu.VMEM((levels, 8, span), F32),
            pltpu.VMEM((2 * group, 1, wide), F32),
            pltpu.VMEM((nq, 1, wide), F32),
            dma((7,)),
            dma((2, nq)), dma((2, nq)), dma((2, nq)), dma((2, nq)),
            dma((group,)), dma((group,)), dma((2, nq)), dma((2, nq)), dma((2,)), dma((2,)),
            dma((2, nq)), dma((2, nq)),
            dma((nz,)), dma((nz,)), dma((nz,)), dma((nz,)),
            dma((2 * group,)), dma((2 * group,)), dma((nq,)), dma((nq,)),
        ],
        compiler_params=pltpu.CompilerParams(
            collective_id=0, has_side_effects=True, vmem_limit_bytes=56 * 2**20
        ),
    )(
        logit_scale.reshape(1, 1), bias, notes, timelines,
        time_days.reshape(1, own), note_days, partner,
    )
    mean_loss, bias_grad, note_grad, time_grad = pl.pallas_call(
        hand_over,
        out_shape=(jax.ShapeDtypeStruct((1,), F32), jax.ShapeDtypeStruct((levels,), F32), grads, grads),
        in_specs=[vmem] * 3,
        out_specs=(vmem,) * 4,
    )(note_grad, time_grad, summary)
    return (mean_loss, bias_grad, note_grad, time_grad)


def solution(mesh):
    placed = (
        P("outer", None),
        P(("outer", "inner"), None),
        P("outer"),
        P("outer"),
        P(("outer", "inner")),
        P(),
        P(),
    )
    return jax.shard_map(
        body,
        mesh=mesh,
        in_specs=placed,
        out_specs=(P(), P(), P(("outer", "inner"), None), P(("outer", "inner"), None)),
        check_vma=False,
    )
```

time: 1000 us -> 88.2 us (0.09)
  the two profiles are of different devices: /device:TPU:192 before, /device:TPU:64 now
where the time goes in v2:
time: 88.2 us; the launch traced here: 88 us
  Pallas kernels  86.7 us (98%)
  between operations  1.29 us (1%)
    pallas_call x1, Pallas kernels, body(): pl.pallas_call(functools.partial(kernel, (nq // ny, ny, nz)), out_shape=(...  85.1 us

profile of v2, /device:TPU:64, one launch (start us, length us, event | category | flops | bytes accessed | tf_op | source)
XLA Modules:
  0.0 88.0 jit_solution(8371042332204196385)
XLA Ops:
  1.3 85.1 %shard_map.102 = (f32[40,512]{1,0:T(8,128)}, f32[40,512]{1,0:T(8,128)}, f32[1,128]{1,0:T(1,128)}) custom-call(f32[1,1]{1,0:T(1,128)} %bitcast.2.scale_any, f32[8]{0:T(128)} %bias_any.1, bf16[640,512]{1,0:T(8,128)(2,1)} %notes_any.1, bf16[40,512]{1,0:T(8,128)(2,1)} %time_any.1, s32[1,40]{1,0:T(1,128)} %bitcast.3, s32[640]{0:T(1024)} %note_when_any.1, ...), custom_call_target="tpu_custom_call" | custom-call | tf_op jit(solution)/shard_map/pallas_call | solution.py:437
  86.4 1.6 %shard_map.103 = (f32[1]{0:T(128)}, f32[8]{0:T(128)}, f32[40,512]{1,0:T(8,128)}, f32[40,512]{1,0:T(8,128)}) custom-call(f32[40,512]{1,0:T(8,128)} %get-tuple-element.7.note_ref, f32[40,512]{1,0:T(8,128)} %get-tuple-element.8.time_ref, f32[1,128]{1,0:T(1,128)} %get-tuple-element.9.summary_ref), custom_call_target="tpu_custom_call" | custom-call | tf_op jit(solution)/shard_map/pallas_call | solution.py:488

commit v3 on v2

--- a/solution.py
+++ b/solution.py
@@ -33,9 +33,9 @@
     scale_ref, bias_ref, notes_ref, note_when_ref, partner_ref,
     shards, shard_days, stage, planes, logits, raws, weights, when_col, partner_col, row_col, spare,
     row_stats, col_stats, col_far, part, time_out, time_in, far_out, far_in,
-    note_near, note_out, note_in, note_own, level_sums, ring_sums, plane_sums,
+    note_near, note_out, note_in, pair_out, pair_in, note_own, level_sums, ring_sums, plane_sums,
     l_sem, g_send, g_recv, d_send, d_recv, r_send, r_recv, c_send, c_recv, f_send, f_recv, t_send, t_recv,
-    n_send, n_recv, m_send, m_recv, a_send, a_recv, b_send, b_recv,
+    n_send, n_recv, m_send, m_recv, p_send, p_recv, a_send, a_recv, b_send, b_recv,
 ):
     nx, ny, nz = sizes
     nq, group = nx * ny, 2 * nz
@@ -92,8 +92,13 @@
     def hello(device):
         pl.semaphore_signal(barrier, inc=1, device_id=device, device_id_type=MESH)
 
+    def hello_far(s, _):
+        hello((q * 2 + 1 - far, inner_peer(s)))
+        return 0
+
+    lax.fori_loop(0, group, hello_far, 0)
+    each(group, lambda s: hello((outer_id, inner_peer(s))))
     each(nq, lambda s: hello(in_plane(plane_peer(s))))
-    each(2 * group, lambda s: hello(on_ring(ring_peer(s))))
 
     loads = [
         pltpu.make_async_copy(src, dst, l_sem.at[k])
@@ -305,7 +310,7 @@
         return pl.ds(pl.multiple_of((2 * k + which) * own, own), own)
 
     def share_core(s):
-        k = lax.rem(line + s, nz)
+        k = lax.rem(line + 2 * s - 1 - (2 * s - 1) // nz * (nz - 1), nz)
         send(note_own.at[chunk(k, 1 - core)], note_near.at[k], n_send.at[k], n_recv.at[k],
              (outer_id, 2 * line + 1 - core))
 
@@ -332,14 +337,32 @@
 
     each(2 * group, share_sums)
 
+    half, odd = line // 2, line % 2
+    beside = (outer_id, 2 * (2 * half + 1 - odd) + core)
+
+    def share_pair(j, _):
+        k = 2 * j + 1 - odd
+        wait_in(note_near.at[k], n_recv.at[k])
+        note_out[j] = (note_own[chunk(k, core)] + note_near[k]).astype(BF16)
+        send(note_out.at[j], note_in.at[j], m_send.at[j], m_recv.at[j], beside)
+        return 0
+
+    lax.fori_loop(0, nz // 2, share_pair, 0)
+
+    def keep_pair(j, _):
+        k = 2 * j + odd
+        wait_in(note_near.at[k], n_recv.at[k])
+        note_near[k] += note_own[chunk(k, core)]
+        return 0
+
+    lax.fori_loop(0, nz // 2, keep_pair, 0)
+
     def share_line(s):
-        k = lax.rem(line + s, nz)
-        wait_in(note_near.at[k], n_recv.at[k])
-        note_out[k] = (note_own[chunk(k, core)] + note_near[k]).astype(BF16)
-        send(note_out.at[k], note_in.at[line], m_send.at[k], m_recv.at[line], (outer_id, 2 * k + core))
-
-    each(nz, share_line)
-    time_partials(0)
+        j = lax.rem(half + s, nz // 2)
+        k = 2 * j + odd
+        wait_in(note_in.at[j], m_recv.at[j])
+        pair_out[j] = (note_near[k] + note_in[j].astype(F32)).astype(BF16)
+        send(pair_out.at[j], pair_in.at[half], p_send.at[j], p_recv.at[half], (outer_id, 2 * k + core))
 
     def time_arrive(plane):
         def one(s):
@@ -351,6 +374,8 @@
     time_arrive(1)
     far_out[...] = part[1].astype(BF16)
     send(far_out, far_in, t_send.at[1, q], t_recv.at[1, q], across)
+    each(nz // 2, share_line)
+    time_partials(0)
 
     def sums_in(s):
         peer = ring_peer(s)
@@ -367,15 +392,15 @@
     time_arrive(0)
 
     factor = scale_ref[...] * F32(1.0 / math.sqrt(depth))
-    wait_in(note_near.at[line], n_recv.at[line])
-    note_near[line] += note_own[chunk(line, core)]
+    wait_in(note_in.at[half], m_recv.at[half])
+    note_near[line] += note_in[half].astype(F32)
 
     def note_arrive(s):
-        k = lax.rem(line + s, nz)
-        wait_in(note_in.at[k], m_recv.at[k])
-        note_near[line] += note_in[k].astype(F32)
-
-    each(nz, note_arrive)
+        j = lax.rem(half + s, nz // 2)
+        wait_in(pair_in.at[j], p_recv.at[j])
+        note_near[line] += pair_in[j].astype(F32)
+
+    each(nz // 2, note_arrive)
     note_grad_ref[...] = factor * note_near[line]
 
     def plane_sums_in(s):
@@ -401,8 +426,8 @@
         wait_out(plane_sums.at[q], b_send.at[peer])
 
     def line_left(s):
-        k = lax.rem(line + s, nz)
-        wait_out(note_out.at[k], m_send.at[k])
+        j = lax.rem(half + s, nz // 2)
+        wait_out(pair_out.at[j], p_send.at[j])
 
     for plane in range(2):
         wait_out(col_far.at[plane], f_send.at[plane])
@@ -410,7 +435,8 @@
     each(group, lambda s: wait_out(row_stats.at[inner_id], r_send.at[inner_peer(s)]))
     each(2 * group, lambda s: wait_out(ring_sums.at[ring_id], a_send.at[ring_peer(s)]))
     each(nz + 1, lambda s: wait_out(note_near.at[0], n_send.at[lax.rem(line + s, nz)]))
-    each(nz, line_left)
+    each(nz // 2, line_left)
+    lax.fori_loop(0, nz // 2, lambda j, _: wait_out(note_out.at[j], m_send.at[j]) or 0, 0)
 
 
 def hand_over(note_ref, time_ref, summary_ref, loss_ref, bias_ref, note_out, time_out):
@@ -465,8 +491,10 @@
             pltpu.VMEM((own, depth), BF16),
             pltpu.VMEM((own, depth), BF16),
             pltpu.VMEM((nz, own, depth), F32),
-            pltpu.VMEM((nz, own, depth), BF16),
-            pltpu.VMEM((nz, own, depth), BF16),
+            pltpu.VMEM((nz // 2, own, depth), BF16),
+            pltpu.VMEM((nz // 2, own, depth), BF16),
+            pltpu.VMEM((nz // 2, own, depth), BF16),
+            pltpu.VMEM((nz // 2, own, depth), BF16),
             pltpu.VMEM((rows, depth), F32),
             pltpu.VMEM((levels, 8, span), F32),
             pltpu.VMEM((2 * group, 1, wide), F32),
@@ -475,7 +503,7 @@
             dma((2, nq)), dma((2, nq)), dma((2, nq)), dma((2, nq)),
             dma((group,)), dma((group,)), dma((2, nq)), dma((2, nq)), dma((2,)), dma((2,)),
             dma((2, nq)), dma((2, nq)),
-            dma((nz,)), dma((nz,)), dma((nz,)), dma((nz,)),
+            dma((nz,)), dma((nz,)), dma((nz // 2,)), dma((nz // 2,)), dma((nz // 2,)), dma((nz // 2,)),
             dma((2 * group,)), dma((2 * group,)), dma((nq,)), dma((nq,)),
         ],
         compiler_params=pltpu.CompilerParams(

time: 88.2 us -> 83.9 us (0.951)
  the two profiles are of different devices: /device:TPU:64 before, /device:TPU:1 now
where the time goes in v3:
time: 83.9 us; the launch traced here: 83.7 us
  Pallas kernels  82.4 us (98%)
  between operations  1.29 us (2%)
    pallas_call x1, Pallas kernels, body(): pl.pallas_call(functools.partial(kernel, (nq // ny, ny, nz)), out_shape=(...  80.8 us

profile of v3, /device:TPU:1, one launch (start us, length us, event | category | flops | bytes accessed | tf_op | source)
XLA Modules:
  0.0 83.7 jit_solution(14388147939665945527)
XLA Ops:
  1.3 80.8 %shard_map.102 = (f32[40,512]{1,0:T(8,128)}, f32[40,512]{1,0:T(8,128)}, f32[1,128]{1,0:T(1,128)}) custom-call(f32[1,1]{1,0:T(1,128)} %bitcast.2.scale_any, f32[8]{0:T(128)} %bias_any.1, bf16[640,512]{1,0:T(8,128)(2,1)} %notes_any.1, bf16[40,512]{1,0:T(8,128)(2,1)} %time_any.1, s32[1,40]{1,0:T(1,128)} %bitcast.3, s32[640]{0:T(1024)} %note_when_any.1, ...), custom_call_target="tpu_custom_call" | custom-call | tf_op jit(solution)/shard_map/pallas_call | solution.py:463
  82.1 1.6 %shard_map.103 = (f32[1]{0:T(128)}, f32[8]{0:T(128)}, f32[40,512]{1,0:T(8,128)}, f32[40,512]{1,0:T(8,128)}) custom-call(f32[40,512]{1,0:T(8,128)} %get-tuple-element.7.note_ref, f32[40,512]{1,0:T(8,128)} %get-tuple-element.8.time_ref, f32[1,128]{1,0:T(1,128)} %get-tuple-element.9.summary_ref), custom_call_target="tpu_custom_call" | custom-call | tf_op jit(solution)/shard_map/pallas_call | solution.py:516

commit v4 on v3

--- a/solution.py
+++ b/solution.py
@@ -109,7 +109,7 @@
     ]
     for load in loads:
         load.start()
-    for load in loads:
+    for load in loads[:2]:
         load.wait()
     pl.semaphore_wait(barrier, (nq - 1) + (2 * group - 1))
 
@@ -125,6 +125,8 @@
         each(nq, one)
 
     share(0)
+    for load in loads[2:]:
+        load.wait()
     scale = scale_ref[...] * F32(LOG2E / math.sqrt(depth))
     lane = lax.broadcasted_iota(jnp.int32, (1, span), 1)
     lane_q = ((lane.astype(F32) + 0.5) * F32(1.0 / own)).astype(jnp.int32)
@@ -315,6 +317,18 @@
              (outer_id, 2 * line + 1 - core))
 
     each(nz + 1, share_core)
+    half, odd = line // 2, line % 2
+    beside = (outer_id, 2 * (2 * half + 1 - odd) + core)
+
+    def share_pair(j, _):
+        k = 2 * j + 1 - odd
+        wait_in(note_near.at[k], n_recv.at[k])
+        note_out[j] = (note_own[chunk(k, core)] + note_near[k]).astype(BF16)
+        send(note_out.at[j], note_in.at[j], m_send.at[j], m_recv.at[j], beside)
+        return 0
+
+    lax.fori_loop(0, nz // 2, share_pair, 0)
+
     add_levels(0, near_days)
 
     above = jnp.sum(level_sums[...], axis=1)
@@ -336,18 +350,6 @@
         send(ring_sums.at[ring_id], ring_sums.at[ring_id], a_send.at[peer], a_recv.at[ring_id], on_ring(peer))
 
     each(2 * group, share_sums)
-
-    half, odd = line // 2, line % 2
-    beside = (outer_id, 2 * (2 * half + 1 - odd) + core)
-
-    def share_pair(j, _):
-        k = 2 * j + 1 - odd
-        wait_in(note_near.at[k], n_recv.at[k])
-        note_out[j] = (note_own[chunk(k, core)] + note_near[k]).astype(BF16)
-        send(note_out.at[j], note_in.at[j], m_send.at[j], m_recv.at[j], beside)
-        return 0
-
-    lax.fori_loop(0, nz // 2, share_pair, 0)
 
     def keep_pair(j, _):
         k = 2 * j + odd

time: 83.9 us -> 82.9 us (0.988)
  Pallas kernels: 82.4 us -> 81.4 us
    pallas_call x1, Pallas kernels: 80.8 us -> 79.8 us  [body(): pl.pallas_call(functools.partial(kernel, (nq // ny, ny, nz)), out_shape=(...]
where the time goes in v4:
time: 82.9 us; the launch traced here: 82.7 us
  Pallas kernels  81.4 us (98%)
  between operations  1.29 us (2%)
    pallas_call x1, Pallas kernels, body(): pl.pallas_call(functools.partial(kernel, (nq // ny, ny, nz)), out_shape=(...  79.8 us

profile of v4, /device:TPU:1, one launch (start us, length us, event | category | flops | bytes accessed | tf_op | source)
XLA Modules:
  0.0 82.7 jit_solution(10752517864779554803)
XLA Ops:
  1.3 79.8 %shard_map.102 = (f32[40,512]{1,0:T(8,128)}, f32[40,512]{1,0:T(8,128)}, f32[1,128]{1,0:T(1,128)}) custom-call(f32[1,1]{1,0:T(1,128)} %bitcast.2.scale_any, f32[8]{0:T(128)} %bias_any.1, bf16[640,512]{1,0:T(8,128)(2,1)} %notes_any.1, bf16[40,512]{1,0:T(8,128)(2,1)} %time_any.1, s32[1,40]{1,0:T(1,128)} %bitcast.3, s32[640]{0:T(1024)} %note_when_any.1, ...), custom_call_target="tpu_custom_call" | custom-call | tf_op jit(solution)/shard_map/pallas_call | solution.py:465
  81.1 1.6 %shard_map.103 = (f32[1]{0:T(128)}, f32[8]{0:T(128)}, f32[40,512]{1,0:T(8,128)}, f32[40,512]{1,0:T(8,128)}) custom-call(f32[40,512]{1,0:T(8,128)} %get-tuple-element.7.note_ref, f32[40,512]{1,0:T(8,128)} %get-tuple-element.8.time_ref, f32[1,128]{1,0:T(1,128)} %get-tuple-element.9.summary_ref), custom_call_target="tpu_custom_call" | custom-call | tf_op jit(solution)/shard_map/pallas_call | solution.py:518

commit v5 on v4

--- a/solution.py
+++ b/solution.py
@@ -183,11 +183,7 @@
             wait_in(shards.at[plane, peer], g_recv.at[plane, peer])
         each(nq, one)
 
-        def settle(k, _):
-            stage[pl.ds(pl.multiple_of(k * own, own), own)] = shards[plane, k].astype(F32)
-            return 0
-        lax.fori_loop(0, nq, settle, 0)
-        planes[plane] = stage[...].astype(BF16)
+        planes[plane] = shards[plane].astype(F32).reshape(span, depth).astype(BF16)
         cols = cols_of(plane)
 
         raws[...] = lax.dot_general(notes_ref[...], planes[plane], (((1,), (1,)), ((), ())),
@@ -228,6 +224,7 @@
         wait_in(col_far.at[2 + plane], f_recv.at[plane])
         return log2_sum([near, col_far[2 + plane]])
 
+    level_sums[...] = jnp.zeros_like(level_sums)
     near_days = days_in(0)
     wait_in(shards.at[1, q], g_recv.at[1, q])
     wait_in(shard_days.at[1, q], d_recv.at[1, q])
@@ -253,7 +250,6 @@
     each(group, rows_in)
     row_log = log2_sum([row_stats[k] for k in range(group)])
     row_col[...] = spread_rows(row_log + 1.0, wide)
-    level_sums[...] = jnp.zeros_like(level_sums)
 
     def weigh(plane, col_log, positive):
         cols = cols_of(plane)

time: 82.9 us -> 82.8 us (level)
  no operation moved by 1% of the time
where the time goes in v5:
time: 82.8 us; the launch traced here: 82.6 us
  Pallas kernels  81.3 us (98%)
  between operations  1.29 us (2%)
    pallas_call x1, Pallas kernels, body(): pl.pallas_call(functools.partial(kernel, (nq // ny, ny, nz)), out_shape=(...  79.7 us

profile of v5, /device:TPU:1, one launch (start us, length us, event | category | flops | bytes accessed | tf_op | source)
XLA Modules:
  0.0 82.6 jit_solution(932123865412894881)
XLA Ops:
  1.3 79.7 %shard_map.102 = (f32[40,512]{1,0:T(8,128)}, f32[40,512]{1,0:T(8,128)}, f32[1,128]{1,0:T(1,128)}) custom-call(f32[1,1]{1,0:T(1,128)} %bitcast.2.scale_any, f32[8]{0:T(128)} %bias_any.1, bf16[640,512]{1,0:T(8,128)(2,1)} %notes_any.1, bf16[40,512]{1,0:T(8,128)(2,1)} %time_any.1, s32[1,40]{1,0:T(1,128)} %bitcast.3, s32[640]{0:T(1024)} %note_when_any.1, ...), custom_call_target="tpu_custom_call" | custom-call | tf_op jit(solution)/shard_map/pallas_call | solution.py:461
  81.0 1.6 %shard_map.103 = (f32[1]{0:T(128)}, f32[8]{0:T(128)}, f32[40,512]{1,0:T(8,128)}, f32[40,512]{1,0:T(8,128)}) custom-call(f32[40,512]{1,0:T(8,128)} %get-tuple-element.7.note_ref, f32[40,512]{1,0:T(8,128)} %get-tuple-element.8.time_ref, f32[1,128]{1,0:T(1,128)} %get-tuple-element.9.summary_ref), custom_call_target="tpu_custom_call" | custom-call | tf_op jit(solution)/shard_map/pallas_call | solution.py:514
